TPU v7x, 32 devices: a whole 2x2x4 slice. The times are simulated.
32 devices in a mesh: rep: 2 (over core), fsdp: 16 (over z, y, x).
Axes of the slice: x: 2, y: 2, z: 4, core: 2. Of those that a mesh axis runs over, the one named last changes fastest.
Arguments:
- anchor: float32 [3584, 7168], P('fsdp'), may hold values from -6 to 6
- momentum: float32 [3584, 7168], P('fsdp', 'rep'), may hold values from -3 to 3
- inner_weight: float32 [2, 3584, 7168], P('rep', 'fsdp'), may hold values from -6 to 6
- first_moment: float32 [2, 3584, 7168], P('rep', 'fsdp'), may hold values from -2 to 2
- second_moment: float32 [2, 3584, 7168], P('rep', 'fsdp'), may hold values from 0.01 to 1
- grad_first: bfloat16 [2, 3584, 7168], P('rep', 'fsdp'), may hold values from -1100 to 1100
- grad_second: bfloat16 [2, 3584, 7168], P('rep', 'fsdp'), may hold values from -1100 to 1100
- outer_step: int32 [1], replicated, may hold values from 0 to 15
Outputs:
- next_anchor: float32 [3584, 7168], P('fsdp')
- next_momentum: float32 [3584, 7168], P('fsdp', 'rep')
- next_inner: float32 [2, 3584, 7168], P('rep', 'fsdp')
- next_first: float32 [2, 3584, 7168], P('rep', 'fsdp')
- next_second: float32 [2, 3584, 7168], P('rep', 'fsdp')
All inputs are finite; a program needn't handle non-finite values.
Results may differ from a plain program's by a relative error of at most 0.0003.
Values sent between devices are 32-bit elements; how exact they have to be, the bound alone decides.
A program may use at most 128 MiB of HBM per device.

v0:
```python
import math

import jax
import jax.numpy as jnp
from jax import lax
from jax.sharding import PartitionSpec as P

D = 3584
FF = 7168


def adam_apply(weight, first_moment, second_moment, grad_full, square_sum, step_count):
    factor = jnp.minimum(1.0, 0.5 * math.sqrt(D * FF) / (jnp.sqrt(square_sum) + 1e-06))
    scaled = factor * grad_full
    first_moment = 0.9 * first_moment + 0.1 * scaled
    second_moment = 0.95 * second_moment + 0.05 * scaled * scaled
    first_hat = first_moment / (1.0 - jnp.power(jnp.float32(0.9), step_count))
    second_hat = second_moment / (1.0 - jnp.power(jnp.float32(0.95), step_count))
    weight = weight - 0.1 * (first_hat / (jnp.sqrt(second_hat) + 1e-08) + 0.1 * weight)
    return (weight, first_moment, second_moment)


def outer_update(anchor, momentum, inner_weight):
    replicas = lax.axis_size("rep")
    col_count = momentum.shape[1]
    col_start = lax.axis_index("rep") * col_count
    pseudo = anchor - inner_weight[0]
    pseudo_sum = lax.psum(pseudo, "rep")
    full_momentum = lax.all_gather(momentum, "rep", axis=1, tiled=True)
    outer_grad = pseudo_sum / replicas
    momentum_full = 0.9 * full_momentum + outer_grad
    next_anchor = anchor - 0.7 * (outer_grad + 0.9 * momentum_full)
    next_momentum = lax.dynamic_slice_in_dim(momentum_full, col_start, col_count, 1)
    return (next_anchor, next_momentum)


def inner_steps(inner_weight, first_moment, second_moment, grad_first, grad_second, outer_step):
    base_step = 2 * outer_step[0]
    grad_one = grad_first[0].astype(jnp.float32)
    grad_two = grad_second[0].astype(jnp.float32)
    weight, moment_one, moment_two = (inner_weight[0], first_moment[0], second_moment[0])
    for offset, grad_full in ((1, grad_one), (2, grad_two)):
        square_sum = lax.psum(jnp.sum(grad_full * grad_full), "fsdp")
        weight, moment_one, moment_two = adam_apply(
            weight,
            moment_one,
            moment_two,
            grad_full,
            square_sum,
            (base_step + offset).astype(jnp.float32),
        )
    return (weight, moment_one, moment_two)


def on_device(
    anchor, momentum, inner_weight, first_moment, second_moment, grad_first, grad_second, outer_step
):
    weight, moment_one, moment_two = inner_steps(
        inner_weight, first_moment, second_moment, grad_first, grad_second, outer_step
    )
    next_anchor, next_momentum = outer_update(anchor, momentum, inner_weight)
    next_inner = (next_anchor + (weight - inner_weight[0]))[None]
    return (next_anchor, next_momentum, next_inner, moment_one[None], moment_two[None])


def solution(mesh):
    in_specs = (
        P("fsdp", None),
        P("fsdp", "rep"),
        P("rep", "fsdp", None),
        P("rep", "fsdp", None),
        P("rep", "fsdp", None),
        P("rep", "fsdp", None),
        P("rep", "fsdp", None),
        P(),
    )
    out_specs = (
        P("fsdp", None),
        P("fsdp", "rep"),
        P("rep", "fsdp", None),
        P("rep", "fsdp", None),
        P("rep", "fsdp", None),
    )
    return jax.shard_map(
        on_device, mesh=mesh, in_specs=in_specs, out_specs=out_specs, check_vma=False
    )
```

profile of v0, /device:TPU:0, one launch (start us, length us, event | category | flops | bytes accessed | tf_op | source)
XLA Modules:
  0.0 108.3 jit_solution(11736036752826426284)
XLA Ops:
  7.2 0.0 all-reduce.3.cloned.1.call-start
  7.2 8.3 %bitcast_subtract_fusion.1 = f32[224,7168]{1,0:T(8,128)} fusion(f32[224,7168]{1,0:T(8,128)} %param.8, f32[1,224,7168]{2,1,0:T(8,128)} %param.10), kind=kLoop, calls=%fused_computation.38 | loop fusion | flops 1605632 | bytes 19267584 | tf_op jit(solution)/shard_map/sub | solution.py:27
  15.5 0.0 copy-start
  15.5 0.0 all-reduce.3.cloned.1.call-update
  15.5 0.0 all-gather.2.cloned.1.call-start
  15.6 0.7 all-gather.2.cloned.1.call-update
  16.3 1.1 %copy-done = bf16[1,224,7168]{2,1,0:T(8,128)(2,1)S(1)} copy-done((bf16[1,224,7168]{2,1,0:T(8,128)(2,1)S(1)}, bf16[1,224,7168]{2,1,0:T(8,128)(2,1)}, u32[]{:S(2)}) %copy-start) | copy-done | bytes 3211288
  17.4 4.2 %fusion.17 = (f32[]{:T(128)}, f32[]{:T(128)}) fusion(bf16[1,224,7168]{2,1,0:T(8,128)(2,1)} %param.13, bf16[1,224,7168]{2,1,0:T(8,128)(2,1)S(1)} %copy-done), kind=kLoop, calls=%fused_computation.25 | loop fusion | flops 9633790 | bytes 6422536 | tf_op jit(solution)/shard_map/reduce_sum | solution.py:43
  21.6 44.1 %all-reduce = (f32[]{:T(128)}, f32[]{:T(128)}) all-reduce(f32[]{:T(128)} %get-tuple-element.13, f32[]{:T(128)} %get-tuple-element.12), channel_id=1, replica_groups=mesh['rep'=2,'fsdp'=16] {'fsdp'}, use_global_device_ids=true, to_apply=%region_4.0 | all-reduce | flops 2 | bytes 16 | tf_op jit(solution)/shard_map/psum | solution.py:43
  68.0 10.2 %fusion.27 = (f32[1,224,7168]{2,1,0:T(8,128)}, f32[1,224,7168]{2,1,0:T(8,128)}) fusion(bf16[1,224,7168]{2,1,0:T(8,128)(2,1)} %param.13, bf16[1,224,7168]{2,1,0:T(8,128)(2,1)S(1)} %copy-done, f32[1,224,7168]{2,1,0:T(8,128)} %param.12, f32[]{:T(128)S(6)} %min.7, f32[]{:T(128)S(6)} %min.6, f32[1,224,7168]{2,1,0:T(8,128)} %param.11), kind=kLoop, calls=%fused_computation.35 | loop fusion | flops 28901376 | bytes 32112648 | tf_op jit(solution)/shard_map/add | solution.py:16
  78.2 0.0 all-reduce.3.cloned.1.call-done
  78.2 0.0 all-gather.2.cloned.1.call-done
  78.2 21.3 %fusion.30 = (f32[1,224,7168]{2,1,0:T(8,128)}, f32[224,7168]{1,0:T(8,128)}, f32[224,7168]{1,0:T(8,128)S(1)}) fusion(bf16[1,224,7168]{2,1,0:T(8,128)(2,1)S(1)} %copy-done, bf16[1,224,7168]{2,1,0:T(8,128)(2,1)} %param.13, f32[1,224,7168]{2,1,0:T(8,128)} %param.10, f32[1,224,7168]{2,1,0:T(8,128)} %param.12, f32[1,224,7168]{2,1,0:T(8,128)} %param.11, ...), kind=kLoop, calls=%fused_computation.43 | loop fusion | flops 69042176 | bytes 64225304 | tf_op jit(solution)/shard_map/broadcast_in_dim | solution.py:62
  99.5 2.0 %constant_dynamic-slice_fusion = f32[224,3584]{1,0:T(8,128)} fusion(f32[224,7168]{1,0:T(8,128)S(1)} %get-tuple-element.9, s32[]{:T(128)S(6)} %select_n.3), kind=kLoop, calls=%fused_computation.44 | loop fusion | bytes 6422532 | tf_op jit(solution)/shard_map/dynamic_slice | solution.py:33
Async XLA Ops:
  7.2 71.0 %all-reduce.3.cloned.1.call-start = ((), (), s32[]{:S(2)}) async-start(), calls=%async_computation | async-start | bytes 12845056 | tf_op jit(solution)/shard_map/psum | solution.py:28
  15.5 1.9 %copy-start = (bf16[1,224,7168]{2,1,0:T(8,128)(2,1)S(1)}, bf16[1,224,7168]{2,1,0:T(8,128)(2,1)}, u32[]{:S(2)}) copy-start(bf16[1,224,7168]{2,1,0:T(8,128)(2,1)} %param.14) | copy-start | bytes 9633796
  15.5 62.6 %all-gather.2.cloned.1.call-start = ((), (), s32[]{:S(2)}) async-start(), calls=%async_computation.1 | async-start | bytes 9633792 | tf_op jit(solution)/shard_map/all_gather | solution.py:29
Sparse Core Ops, SparseCore 0:
  15.7 35.0 all-reduce.2
  52.4 18.1 all-gather.1
where the time goes:
time: 109 us; the launch traced here: 108 us
  blocking collectives  44.1 us (40%)
  other arithmetic  43.9 us (40%)
  between operations  16.3 us (15%)
  local copies, waits for them, and re-layouts  3.1 us (3%)
    psum x1, blocking collectives, inner_steps(): square_sum = lax.psum(jnp.sum(grad_full * grad_full), 'fsdp')  44.1 us
    broadcast_in_dim x1, other arithmetic, on_device(): next_inner = (next_anchor + (weight - inner_weight[0]))[None]  21.3 us
    add x1, other arithmetic, adam_apply(): second_moment = 0.95 * second_moment + 0.05 * scaled * scaled  10.2 us
    sub x1, other arithmetic, outer_update(): pseudo = anchor - inner_weight[0]  8.31 us
    reduce_sum x1, other arithmetic, inner_steps(): square_sum = lax.psum(jnp.sum(grad_full * grad_full), 'fsdp')  4.17 us
  transfers between devices with their start and end apart: 2, of which 0 were waited for; matrix products, arithmetic and copies ran while one was open for 13% of the time, Pallas kernels for 0%

commit v1 on v0

--- a/solution.py
+++ b/solution.py
@@ -1,12 +1,20 @@
+import functools
 import math
 
 import jax
 import jax.numpy as jnp
 from jax import lax
+from jax.experimental import pallas as pl
+from jax.experimental.pallas import tpu as pltpu
 from jax.sharding import PartitionSpec as P
 
 D = 3584
 FF = 7168
+CHUNK = 32
+ROWS = 16
+COLS = 256
+SLOTS = 4
+MESH = pl.DeviceIdType.MESH
 
 
 def adam_apply(weight, first_moment, second_moment, grad_full, square_sum, step_count):
@@ -52,7 +60,7 @@
     return (weight, moment_one, moment_two)
 
 
-def on_device(
+def plain(
     anchor, momentum, inner_weight, first_moment, second_moment, grad_first, grad_second, outer_step
 ):
     weight, moment_one, moment_two = inner_steps(
@@ -63,6 +71,282 @@
     return (next_anchor, next_momentum, next_inner, moment_one[None], moment_two[None])
 
 
+def exchange_kernel(
+    peers,
+    anchor, momentum, inner, first, second, grad_one, grad_two,
+    na, nm, w, m, v, g1, g2, sums,
+    other_w, gathered,
+    g1_sem, g2_sem, a_sem, w_sem, mom_sem, bulk_sem,
+    w_send, w_recv, na_send, na_recv, s_send, s_recv,
+):
+    rows, half = momentum.shape
+    chunks = rows // CHUNK
+    me = lax.axis_index("fsdp")
+    rep = lax.axis_index("rep")
+    partner = 1 - rep
+    own = pl.ds(pl.multiple_of(rep * half, 128), half)
+    far = pl.ds(pl.multiple_of(partner * half, 128), half)
+
+    def cut(i):
+        return pl.ds(i * CHUNK, CHUNK)
+
+    barrier = pltpu.get_barrier_semaphore()
+    pl.semaphore_signal(barrier, inc=1, device_id={"rep": partner}, device_id_type=MESH)
+    for d in range(1, peers):
+        pl.semaphore_signal(
+            barrier, inc=1, device_id={"fsdp": lax.rem(me + d, peers)}, device_id_type=MESH
+        )
+
+    g1_in = [pltpu.make_async_copy(grad_one.at[0, cut(i)], g1.at[cut(i)], g1_sem.at[i]) for i in range(chunks)]
+    g2_in = [pltpu.make_async_copy(grad_two.at[0, cut(i)], g2.at[cut(i)], g2_sem.at[i]) for i in range(chunks)]
+    a_in = [pltpu.make_async_copy(anchor.at[cut(i), own], na.at[cut(i), own], a_sem.at[i]) for i in range(chunks)]
+    w_in = [pltpu.make_async_copy(inner.at[0, cut(i), own], w.at[cut(i), own], w_sem.at[i]) for i in range(chunks)]
+    mom_in = [pltpu.make_async_copy(momentum.at[cut(i)], nm.at[cut(i)], mom_sem.at[i]) for i in range(chunks)]
+    bulk = [
+        pltpu.make_async_copy(inner.at[0, :, far], w.at[:, far], bulk_sem.at[0]),
+        pltpu.make_async_copy(first.at[0], m, bulk_sem.at[1]),
+        pltpu.make_async_copy(second.at[0], v, bulk_sem.at[2]),
+    ]
+    for i in range(chunks):
+        g1_in[i].start()
+        g2_in[i].start()
+    for i in range(chunks):
+        a_in[i].start()
+        w_in[i].start()
+        mom_in[i].start()
+
+    pl.semaphore_wait(barrier, peers)
+
+    w_out = [
+        pltpu.make_async_remote_copy(
+            src_ref=inner.at[0, cut(i), far], dst_ref=other_w.at[cut(i)],
+            send_sem=w_send.at[i], recv_sem=w_recv.at[i],
+            device_id={"rep": partner}, device_id_type=MESH,
+        )
+        for i in range(chunks)
+    ]
+    for c in w_out:
+        c.start()
+    for c in bulk:
+        c.start()
+
+    lane = 128
+    tiles = (2 * half) // lane
+    total1 = total2 = jnp.zeros((8, lane), jnp.float32)
+    for i in range(chunks):
+        g1_in[i].wait()
+        g2_in[i].wait()
+
+        def square(j, carry):
+            base = pl.multiple_of(i * CHUNK + j * ROWS, ROWS)
+            accs = list(carry)
+            for t in range(tiles):
+                for k, ref in ((0, g1), (2, g2)):
+                    x = ref[pl.ds(base, ROWS), t * lane:(t + 1) * lane].astype(jnp.float32)
+                    x = x * x
+                    accs[k] = accs[k] + x[:8]
+                    accs[k + 1] = accs[k + 1] + x[8:]
+            return tuple(accs)
+
+        zero = jnp.zeros((8, lane), jnp.float32)
+        accs = lax.fori_loop(0, CHUNK // ROWS, square, (zero,) * 4)
+        total1 = total1 + (accs[0] + accs[1])
+        total2 = total2 + (accs[2] + accs[3])
+
+    gathered[me, 0] = total1
+    gathered[me, 1] = total2
+    s_out = []
+    for d in range(1, peers):
+        c = pltpu.make_async_remote_copy(
+            src_ref=gathered.at[me], dst_ref=gathered.at[me],
+            send_sem=s_send.at[d], recv_sem=s_recv.at[me],
+            device_id={"fsdp": lax.rem(me + d, peers)}, device_id_type=MESH,
+        )
+        c.start()
+        s_out.append(c)
+
+    na_out = []
+    for i in range(chunks):
+        a_in[i].wait()
+        w_in[i].wait()
+        mom_in[i].wait()
+        w_out[i].wait_recv()
+
+        def outer(j, carry):
+            base = pl.multiple_of(i * CHUNK + j * 8, 8)
+            rs = pl.ds(base, 8)
+            for t in range(0, half, COLS):
+                cs = pl.ds(pl.multiple_of(rep * half + t, 128), COLS)
+                a = na[rs, cs]
+                grad = ((a - w[rs, cs]) + (a - other_w[rs, t:t + COLS])) * 0.5
+                mom = 0.9 * nm[rs, t:t + COLS] + grad
+                nm[rs, t:t + COLS] = mom
+                na[rs, cs] = a - 0.7 * (grad + 0.9 * mom)
+            return carry
+
+        lax.fori_loop(0, CHUNK // 8, outer, 0)
+        c = pltpu.make_async_remote_copy(
+            src_ref=na.at[cut(i), own], dst_ref=na.at[cut(i), own],
+            send_sem=na_send.at[i], recv_sem=na_recv.at[i],
+            device_id={"rep": partner}, device_id_type=MESH,
+        )
+        c.start()
+        na_out.append(c)
+
+    for d in range(1, peers):
+        src = lax.rem(me + d, peers)
+        pltpu.make_async_remote_copy(
+            src_ref=gathered.at[src], dst_ref=gathered.at[src],
+            send_sem=s_send.at[d], recv_sem=s_recv.at[src],
+            device_id={"fsdp": src}, device_id_type=MESH,
+        ).wait_recv()
+    for c in s_out:
+        c.wait_send()
+    t1, t2 = gathered[0, 0], gathered[0, 1]
+    for d in range(1, peers):
+        t1 = t1 + gathered[d, 0]
+        t2 = t2 + gathered[d, 1]
+    sums[0] = t1
+    sums[1] = t2
+    for c in bulk:
+        c.wait()
+    for i in range(chunks):
+        w_out[i].wait_send()
+        na_out[i].wait()
+
+
+def adam_kernel(
+    numel,
+    step, na, nm, w, m, v, g1, g2, sums,
+    na_out, nm_out, ni_out, nf_out, ns_out,
+    ni, nf, ns, sem,
+):
+    na_copy = pltpu.make_async_copy(na, na_out, sem.at[0, 0])
+    nm_copy = pltpu.make_async_copy(nm, nm_out, sem.at[1, 0])
+    na_copy.start()
+    nm_copy.start()
+    rows, cols = w.shape
+
+    def scalars(k):
+        square_sum = jnp.sum(sums[k])
+        norm = jnp.sqrt(jnp.full((8, 128), square_sum, jnp.float32))
+        factor = jnp.minimum(1.0, 0.5 * math.sqrt(numel) / (norm + 1e-06))
+        t = jnp.full((8, 128), 2 * step[0] + (k + 1), jnp.int32).astype(jnp.float32)
+        b1 = 1.0 - jnp.exp(t * math.log(0.9))
+        b2 = jnp.sqrt(1.0 - jnp.exp(t * math.log(0.95)))
+        return (0.1 * factor)[0, 0], (0.1 * b2 / b1)[0, 0], (1e-08 * b2)[0, 0]
+
+    h1, k1, e1 = scalars(0)
+    h2, k2, e2 = scalars(1)
+    k1 = k1 * 0.99
+
+    triples = ((ni, ni_out), (nf, nf_out), (ns, ns_out))
+
+    def copies(j):
+        slot = lax.rem(j, SLOTS)
+        rs = pl.ds(pl.multiple_of(j * ROWS, ROWS), ROWS)
+        return [
+            pltpu.make_async_copy(src.at[slot], dst.at[0, rs], sem.at[2 + k, slot])
+            for k, (src, dst) in enumerate(triples)
+        ]
+
+    def body(j, carry):
+        slot = lax.rem(j, SLOTS)
+
+        @pl.when(j >= SLOTS)
+        def _():
+            for c in copies(j - SLOTS):
+                c.wait()
+
+        rs = pl.ds(pl.multiple_of(j * ROWS, ROWS), ROWS)
+        for c in range(0, cols, COLS):
+            cs = slice(c, c + COLS)
+            x = h1 * g1[rs, cs].astype(jnp.float32)
+            mm = 0.9 * m[rs, cs] + x
+            vv = 0.95 * v[rs, cs] + 5.0 * (x * x)
+            d = vv * lax.rsqrt(vv) + e1
+            up = (k1 * mm) * lax.rsqrt(d * d)
+            x = h2 * g2[rs, cs].astype(jnp.float32)
+            mm = 0.9 * mm + x
+            vv = 0.95 * vv + 5.0 * (x * x)
+            nf[slot, :, cs] = mm
+            ns[slot, :, cs] = vv
+            d = vv * lax.rsqrt(vv) + e2
+            up = up + (k2 * mm) * lax.rsqrt(d * d)
+            ni[slot, :, cs] = na[rs, cs] - (0.0199 * w[rs, cs] + up)
+        for c in copies(j):
+            c.start()
+        return carry
+
+    steps = rows // ROWS
+    lax.fori_loop(0, steps, body, 0)
+    for j in range(max(0, steps - SLOTS), steps):
+        for c in copies(j):
+            c.wait()
+    na_copy.wait()
+    nm_copy.wait()
+
+
+def fused(
+    numel, peers,
+    anchor, momentum, inner_weight, first_moment, second_moment, grad_first, grad_second, outer_step,
+):
+    rows, cols = anchor.shape
+    half = momentum.shape[1]
+    chunks = rows // CHUNK
+    f32, bf16 = jnp.float32, jnp.bfloat16
+    hbm = pl.BlockSpec(memory_space=pl.ANY)
+    vmem = pl.BlockSpec(memory_space=pltpu.VMEM)
+    dma = pltpu.SemaphoreType.DMA
+    held = pl.pallas_call(
+        functools.partial(exchange_kernel, peers),
+        name="exchange",
+        out_shape=[
+            pltpu.VMEM((rows, cols), f32),
+            pltpu.VMEM((rows, half), f32),
+            pltpu.VMEM((rows, cols), f32),
+            pltpu.VMEM((rows, cols), f32),
+            pltpu.VMEM((rows, cols), f32),
+            pltpu.VMEM((rows, cols), bf16),
+            pltpu.VMEM((rows, cols), bf16),
+            pltpu.VMEM((2, 8, 128), f32),
+        ],
+        in_specs=[hbm] * 7,
+        out_specs=[vmem] * 8,
+        scratch_shapes=[
+            pltpu.VMEM((rows, half), f32),
+            pltpu.VMEM((peers, 2, 8, 128), f32),
+            dma((chunks,)), dma((chunks,)), dma((chunks,)), dma((chunks,)), dma((chunks,)),
+            dma((3,)),
+            dma((chunks,)), dma((chunks,)), dma((chunks,)), dma((chunks,)),
+            dma((peers,)), dma((peers,)),
+        ],
+        compiler_params=pltpu.CompilerParams(
+            collective_id=0, has_side_effects=True, vmem_limit_bytes=VMEM_A
+        ),
+    )(anchor, momentum, inner_weight, first_moment, second_moment, grad_first, grad_second)
+    out = jax.ShapeDtypeStruct
+    return pl.pallas_call(
+        functools.partial(adam_kernel, numel),
+        name="adam",
+        out_shape=[
+            out((rows, cols), f32),
+            out((rows, half), f32),
+            out((1, rows, cols), f32),
+            out((1, rows, cols), f32),
+            out((1, rows, cols), f32),
+        ],
+        in_specs=[pl.BlockSpec(memory_space=pltpu.SMEM)] + [vmem] * 8,
+        out_specs=[hbm] * 5,
+        scratch_shapes=[pltpu.VMEM((SLOTS, ROWS, cols), f32)] * 3 + [dma((5, SLOTS))],
+        compiler_params=pltpu.CompilerParams(vmem_limit_bytes=VMEM_B),
+    )(outer_step, *(pltpu.with_memory_space_constraint(x, pltpu.VMEM) for x in held))
+
+
+VMEM_A = 8 << 20
+VMEM_B = 8 << 20
+
+
 def solution(mesh):
     in_specs = (
         P("fsdp", None),
@@ -81,6 +365,14 @@
         P("rep", "fsdp", None),
         P("rep", "fsdp", None),
     )
+    reps, peers = mesh.shape["rep"], mesh.shape["fsdp"]
+
+    def on_device(*args):
+        rows, cols = args[0].shape
+        if reps == 2 and rows % CHUNK == 0 and cols % (2 * COLS) == 0:
+            return tuple(fused(rows * peers * cols, peers, *args))
+        return plain(*args)
+
     return jax.shard_map(
         on_device, mesh=mesh, in_specs=in_specs, out_specs=out_specs, check_vma=False
     )

time: 109 us -> 36.4 us (0.33)
  blocking collectives: 44.1 us -> 0 us
  other arithmetic: 43.9 us -> 0 us
  Pallas kernels: 0 us -> 29.2 us
  between operations: 16.3 us -> 1.3 us
  local copies, waits for them, and re-layouts: 3.1 us -> 5.72 us
    psum x1 -> x0, blocking collectives: 44.1 us -> none  [inner_steps(): square_sum = lax.psum(jnp.sum(grad_full * grad_full), 'fsdp')]
    pallas_call x0 -> x2, Pallas kernels: none -> 29.2 us  [the longest x1 17.8 us: fused(): pl.pallas_call(functools.partial(exchange_kernel, peers), name='exchange'...]
    broadcast_in_dim x1 -> x0, other arithmetic: 21.3 us -> none  [on_device(): next_inner = (next_anchor + (weight - inner_weight[0]))[None]]
    add x1 -> x0, other arithmetic: 10.2 us -> none  [adam_apply(): second_moment = 0.95 * second_moment + 0.05 * scaled * scaled]
    sub x1 -> x0, other arithmetic: 8.31 us -> none  [outer_update(): pseudo = anchor - inner_weight[0]]
    unnamed x2 -> x6, local copies, waits for them, and re-layouts: 1.13 us -> 5.72 us
    reduce_sum x1 -> x0, other arithmetic: 4.17 us -> none  [inner_steps(): square_sum = lax.psum(jnp.sum(grad_full * grad_full), 'fsdp')]
    dynamic_slice x1 -> x0, local copies, waits for them, and re-layouts: 1.96 us -> none  [outer_update(): lax.dynamic_slice_in_dim(momentum_full, col_start, col_count, 1)]
  transfers between devices with their start and end apart: 2 -> 0, of which waited for: 0 -> 0; matrix products, arithmetic and copies ran while one was open for 13% -> 0% of each run, Pallas kernels for 0% -> 0%
where the time goes in v1:
time: 36.4 us; the launch traced here: 36.2 us
  Pallas kernels  29.2 us (80%)
  local copies, waits for them, and re-layouts  5.72 us (16%)
  between operations  1.3 us (4%)
    pallas_call x1, Pallas kernels, fused(): pl.pallas_call(functools.partial(exchange_kernel, peers), name='exchange'...  17.8 us
    pallas_call x1, Pallas kernels, fused(): pl.pallas_call(functools.partial(adam_kernel, numel), name='adam', out_sh...  11.4 us
    unnamed x6, local copies, waits for them, and re-layouts  5.72 us

profile of v1, /device:TPU:0, one launch (start us, length us, event | category | flops | bytes accessed | tf_op | source)
XLA Modules:
  0.0 36.2 jit_solution(14855947786572842277)
XLA Ops:
  1.3 0.0 copy-start
  1.3 1.9 %copy-done = f32[224,3584]{1,0:T(8,128)S(1)} copy-done((f32[224,3584]{1,0:T(8,128)S(1)}, f32[224,3584]{1,0:T(8,128)}, u32[]{:S(2)}) %copy-start) | copy-done | bytes 3211288
  3.2 0.0 copy-start.1
  3.2 1.9 %copy-done.1 = bf16[1,224,7168]{2,1,0:T(8,128)(2,1)S(1)} copy-done((bf16[1,224,7168]{2,1,0:T(8,128)(2,1)S(1)}, bf16[1,224,7168]{2,1,0:T(8,128)(2,1)}, u32[]{:S(2)}) %copy-start.1) | copy-done | bytes 3211288
  5.1 0.0 copy-start.2
  5.1 1.9 %copy-done.2 = bf16[1,224,7168]{2,1,0:T(8,128)(2,1)S(1)} copy-done((bf16[1,224,7168]{2,1,0:T(8,128)(2,1)S(1)}, bf16[1,224,7168]{2,1,0:T(8,128)(2,1)}, u32[]{:S(2)}) %copy-start.2) | copy-done | bytes 3211288
  7.0 17.8 %exchange.1 = (f32[224,7168]{1,0:T(8,128)S(1)}, f32[224,3584]{1,0:T(8,128)S(1)}, f32[224,7168]{1,0:T(8,128)S(1)}, f32[224,7168]{1,0:T(8,128)S(1)}, f32[224,7168]...) custom-call(f32[224,7168]{1,0:T(8,128)} %anchor.1, ...), custom_call_target="tpu_custom_call" | custom-call | tf_op jit(solution)/shard_map/exchange/pallas_call | solution.py:301
  24.8 11.4 %adam.1 = (f32[224,7168]{1,0:T(8,128)}, f32[224,3584]{1,0:T(8,128)}, f32[1,224,7168]{2,1,0:T(8,128)}, f32[1,224,7168]{2,1,0:T(8,128)}, f32[1,224,7168]{2,1,0:T(8,128)}) custom-call(s32[1]{0:T(128)S(6)} %copy.13.step, f32[224,7168]{1,0:T(8,128)S(1)} %get-tuple-element.13.na, f32[224,3584]{1,0:T(8,128)S(1)} %get-tuple-element.14.nm, ...), custom_call_target="tpu_custom_call" | custom-call | tf_op jit(solution)/shard_map/adam/pallas_call | solution.py:329
Async XLA Ops:
  1.3 1.9 %copy-start = (f32[224,3584]{1,0:T(8,128)S(1)}, f32[224,3584]{1,0:T(8,128)}, u32[]{:S(2)}) copy-start(f32[224,3584]{1,0:T(8,128)} %momentum.1) | copy-start | bytes 9633796
  3.2 1.9 %copy-start.1 = (bf16[1,224,7168]{2,1,0:T(8,128)(2,1)S(1)}, bf16[1,224,7168]{2,1,0:T(8,128)(2,1)}, u32[]{:S(2)}) copy-start(bf16[1,224,7168]{2,1,0:T(8,128)(2,1)} %grad_one.1) | copy-start | bytes 9633796
  5.1 1.9 %copy-start.2 = (bf16[1,224,7168]{2,1,0:T(8,128)(2,1)S(1)}, bf16[1,224,7168]{2,1,0:T(8,128)(2,1)}, u32[]{:S(2)}) copy-start(bf16[1,224,7168]{2,1,0:T(8,128)(2,1)} %grad_two.1) | copy-start | bytes 9633796

commit v2 on v1

--- a/solution.py
+++ b/solution.py
@@ -324,7 +324,9 @@
         compiler_params=pltpu.CompilerParams(
             collective_id=0, has_side_effects=True, vmem_limit_bytes=VMEM_A
         ),
-    )(anchor, momentum, inner_weight, first_moment, second_moment, grad_first, grad_second)
+    )(*(pltpu.with_memory_space_constraint(x, pltpu.HBM) for x in (
+        anchor, momentum, inner_weight, first_moment, second_moment, grad_first, grad_second
+    )))
     out = jax.ShapeDtypeStruct
     return pl.pallas_call(
         functools.partial(adam_kernel, numel),

time: 36.4 us -> 30.6 us (0.84)
  local copies, waits for them, and re-layouts: 5.72 us -> 0 us
    unnamed x6 -> x0, local copies, waits for them, and re-layouts: 5.72 us -> none
where the time goes in v2:
time: 30.6 us; the launch traced here: 30.5 us
  Pallas kernels  29.2 us (95%)
  between operations  1.29 us (4%)
    pallas_call x1, Pallas kernels, fused(): pl.pallas_call(functools.partial(exchange_kernel, peers), name='exchange'...  17.8 us
    pallas_call x1, Pallas kernels, fused(): pl.pallas_call(functools.partial(adam_kernel, numel), name='adam', out_sh...  11.3 us

profile of v2, /device:TPU:0, one launch (start us, length us, event | category | flops | bytes accessed | tf_op | source)
XLA Modules:
  0.0 30.5 jit_solution(14434460554772975517)
XLA Ops:
  1.3 17.8 %exchange.1 = (f32[224,7168]{1,0:T(8,128)S(1)}, f32[224,3584]{1,0:T(8,128)S(1)}, f32[224,7168]{1,0:T(8,128)S(1)}, f32[224,7168]{1,0:T(8,128)S(1)}, f32[224,7168]...) custom-call(f32[224,7168]{1,0:T(8,128)} %anchor.1, ...), custom_call_target="tpu_custom_call" | custom-call | tf_op jit(solution)/shard_map/exchange/pallas_call | solution.py:301
  19.1 11.3 %adam.1 = (f32[224,7168]{1,0:T(8,128)}, f32[224,3584]{1,0:T(8,128)}, f32[1,224,7168]{2,1,0:T(8,128)}, f32[1,224,7168]{2,1,0:T(8,128)}, f32[1,224,7168]{2,1,0:T(8,128)}) custom-call(s32[1]{0:T(128)S(6)} %copy.13.step, f32[224,7168]{1,0:T(8,128)S(1)} %get-tuple-element.13.na, f32[224,3584]{1,0:T(8,128)S(1)} %get-tuple-element.14.nm, ...), custom_call_target="tpu_custom_call" | custom-call | tf_op jit(solution)/shard_map/adam/pallas_call | solution.py:331
